TPU v7x, 32 devices: a whole 2x2x4 slice. The times are simulated.
32 devices in a mesh: dp: 8 (over z, core), ctx: 4 (over y, x).
Axes of the slice: x: 2, y: 2, z: 4, core: 2. Of those that a mesh axis runs over, the one named last changes fastest.
Arguments:
- inputs: bfloat16 [4096, 8192], P(('dp', 'ctx')), may hold values from -6 to 6
- out_grad: bfloat16 [4096, 8192], P(('dp', 'ctx')), may hold values from -6 to 6
- queries: bfloat16 [4096, 1024], P(('dp', 'ctx')), may hold values from -9 to 9
- keys: bfloat16 [4096, 128], P(('dp', 'ctx')), may hold values from -9 to 9
- values: bfloat16 [4096, 128], P(('dp', 'ctx')), may hold values from -6 to 6
- attn_grad: bfloat16 [4096, 1024], P(('dp', 'ctx')), may hold values from -6 to 6
- doc_lengths: int32 [8, 12], P('dp'), may hold values from 1 to 256, 512 in all within a row
- block_owner: int32 [8, 16], P('dp'), may hold values from 0 to 3, as said below
- basis_qkv: bfloat16 [8192, 512], P('ctx'), may hold values from -0.0625 to 0.0625
- basis_out: bfloat16 [8192, 512], P('ctx'), may hold values from -0.0625 to 0.0625
Outputs:
- grad_queries: bfloat16 [4096, 1024], P(('dp', 'ctx'))
- grad_keys: bfloat16 [4096, 128], P(('dp', 'ctx'))
- grad_values: bfloat16 [4096, 128], P(('dp', 'ctx'))
- galore_qkv: float32 [512, 1280], P(('dp', 'ctx'))
- galore_out: float32 [512, 1024], P(('dp', 'ctx'))
Inputs may be any that keep to these rules, and one draw needn't show every extreme that they name: `block_owner`: in each window every ctx device is named by exactly 4 blocks, and by at most one of the 4 consecutive blocks of any one device.
All inputs are finite; a program needn't handle non-finite values.
Results may differ from a plain program's by a relative error of at most 0.018.
Values may be sent and summed in bfloat16 or wider, within the bound.
A program may use at most 128 MiB of HBM per device.

v0:
```python
import math

import jax
import jax.numpy as jnp
from jax import lax
from jax.sharding import PartitionSpec as P

HD = 128
HQ = 8
GROUPS = 1
BPD = 4


NEG_LARGE = -1e30


def doc_index_of(ends_row, positions):
    return jnp.sum((positions[:, None] >= ends_row[None, :]).astype(jnp.int32), axis=1)


def doc_start_of(ends_row, position):
    return jnp.max(jnp.where(ends_row <= position, ends_row, 0))


def slot_buffer(blocks, destination, peer_count):
    chooser = (destination[None, :] == jnp.arange(peer_count, dtype=jnp.int32)[:, None]).astype(
        blocks.dtype
    )
    return jnp.einsum("dj,jbf->dbf", chooser, blocks)


def compact_slots(received, sources, peer_count):
    chooser = (sources[:, None] == jnp.arange(peer_count, dtype=jnp.int32)[None, :]).astype(
        received.dtype
    )
    return jnp.einsum("kd,dbf->kbf", chooser, received)


def attend_group(
    query_rows,
    dout_rows,
    row_pos,
    row_docs,
    low_key,
    high_key,
    key_group,
    value_group,
    key_docs,
    key_block,
    grad_key,
    grad_value,
):
    scale_factor = HD ** (-0.5)
    block_count = key_group.shape[0] // key_block
    row_count = query_rows.shape[0]
    across = (((1,), (1,)), ((), ()))
    downward = (((0,), (0,)), ((), ()))

    def block_scores(block_id):
        begin_key = block_id * key_block
        key_piece = lax.dynamic_slice_in_dim(key_group, begin_key, key_block, 0)
        value_piece = lax.dynamic_slice_in_dim(value_group, begin_key, key_block, 0)
        piece_docs = lax.dynamic_slice_in_dim(key_docs, begin_key, key_block, 0)
        key_pos = begin_key + jnp.arange(key_block, dtype=jnp.int32)
        allowed = (row_docs[:, None] == piece_docs[None, :]) & (
            key_pos[None, :] <= row_pos[:, None]
        )
        scores = (
            lax.dot_general(query_rows, key_piece, across, preferred_element_type=jnp.float32)
            * scale_factor
        )
        return (scores, allowed, key_piece, value_piece)

    def needed(block_id):
        return (block_id * key_block <= high_key) & ((block_id + 1) * key_block > low_key)

    def stats_step(block_id, running):

        def stats_compute(stats_in):
            peak_old, total_old = stats_in
            scores, allowed, key_piece, value_piece = block_scores(block_id)
            peak_new = jnp.maximum(peak_old, jnp.max(jnp.where(allowed, scores, NEG_LARGE), axis=1))
            shifted = jnp.where(allowed, jnp.exp(scores - peak_new[:, None]), 0.0)
            return (peak_new, total_old * jnp.exp(peak_old - peak_new) + jnp.sum(shifted, axis=1))

        return lax.cond(needed(block_id), stats_compute, lambda unchanged: unchanged, running)

    start_stats = (
        jnp.full((row_count,), NEG_LARGE, jnp.float32),
        jnp.zeros((row_count,), jnp.float32),
    )
    peak_score, denom_total = lax.fori_loop(0, block_count, stats_step, start_stats)
    log_total = peak_score + jnp.log(denom_total)

    def out_step(block_id, running):

        def out_compute(acc_in):
            scores, allowed, key_piece, value_piece = block_scores(block_id)
            weights = jnp.where(allowed, jnp.exp(scores - log_total[:, None]), 0.0).astype(
                jnp.bfloat16
            )
            return acc_in + jnp.dot(weights, value_piece, preferred_element_type=jnp.float32)

        return lax.cond(needed(block_id), out_compute, lambda unchanged: unchanged, running)

    out_sums = lax.fori_loop(0, block_count, out_step, jnp.zeros((row_count, HD), jnp.float32))
    out_rows = out_sums.astype(jnp.bfloat16)
    row_delta = jnp.sum(dout_rows.astype(jnp.float32) * out_rows.astype(jnp.float32), axis=1)

    def grad_step(block_id, running):

        def grad_compute(carried):
            grad_query, key_acc, value_acc = carried
            scores, allowed, key_piece, value_piece = block_scores(block_id)
            probability = jnp.where(allowed, jnp.exp(scores - log_total[:, None]), 0.0)
            weights = probability.astype(jnp.bfloat16)
            grad_prob = lax.dot_general(
                dout_rows, value_piece, across, preferred_element_type=jnp.float32
            )
            grad_scores = (probability * (grad_prob - row_delta[:, None]) * scale_factor).astype(
                jnp.bfloat16
            )
            grad_query = grad_query + jnp.dot(
                grad_scores, key_piece, preferred_element_type=jnp.float32
            )
            begin_key = block_id * key_block
            key_update = lax.dot_general(
                grad_scores, query_rows, downward, preferred_element_type=jnp.float32
            )
            value_update = lax.dot_general(
                weights, dout_rows, downward, preferred_element_type=jnp.float32
            )
            key_acc = lax.dynamic_update_slice_in_dim(
                key_acc,
                lax.dynamic_slice_in_dim(key_acc, begin_key, key_block, 0) + key_update,
                begin_key,
                0,
            )
            value_acc = lax.dynamic_update_slice_in_dim(
                value_acc,
                lax.dynamic_slice_in_dim(value_acc, begin_key, key_block, 0) + value_update,
                begin_key,
                0,
            )
            return (grad_query, key_acc, value_acc)

        return lax.cond(needed(block_id), grad_compute, lambda unchanged: unchanged, running)

    start_grads = (jnp.zeros((row_count, HD), jnp.float32), grad_key, grad_value)
    grad_query, grad_key, grad_value = lax.fori_loop(0, block_count, grad_step, start_grads)
    return (grad_query.astype(jnp.bfloat16), out_rows, grad_key, grad_value)


def attention_backward(
    query_local, dout_local, block_starts, key_all, value_all, ends_row, block_len, key_block
):
    token_count = query_local.shape[0]
    window_len = key_all.shape[0]
    key_docs = doc_index_of(ends_row, jnp.arange(window_len, dtype=jnp.int32))
    query_view = query_local.reshape(token_count, GROUPS, HQ * HD)
    dout_view = dout_local.reshape(token_count, GROUPS, HQ * HD)
    query_groups, out_groups, key_groups, value_groups = ([], [], [], [])
    grad_key = jnp.zeros((window_len, HD), jnp.float32)
    grad_value = jnp.zeros((window_len, HD), jnp.float32)
    query_blocks = []
    out_blocks = []
    for block_id in range(BPD):
        first_pos = block_starts[block_id]
        lower_row = block_id * block_len
        query_rows = query_view[lower_row : lower_row + block_len, 0].reshape(block_len * HQ, HD)
        dout_rows = dout_view[lower_row : lower_row + block_len, 0].reshape(block_len * HQ, HD)
        row_pos = jnp.repeat(first_pos + jnp.arange(block_len, dtype=jnp.int32), HQ)
        row_docs = doc_index_of(ends_row, row_pos)
        low_key = doc_start_of(ends_row, first_pos)
        high_key = first_pos + block_len - 1
        grad_rows, out_rows, grad_key, grad_value = attend_group(
            query_rows,
            dout_rows,
            row_pos,
            row_docs,
            low_key,
            high_key,
            key_all,
            value_all,
            key_docs,
            key_block,
            grad_key,
            grad_value,
        )
        query_blocks.append(grad_rows.reshape(block_len, HQ * HD))
        out_blocks.append(out_rows.reshape(block_len, HQ * HD))
    query_groups.append(jnp.concatenate(query_blocks, axis=0))
    out_groups.append(jnp.concatenate(out_blocks, axis=0))
    key_groups.append(grad_key)
    value_groups.append(grad_value)
    return (query_groups[0], out_groups[0], key_groups[0], value_groups[0])


def shards(
    inputs,
    out_grad,
    queries,
    keys,
    values,
    attn_grad,
    doc_lengths,
    block_owner,
    basis_qkv,
    basis_out,
):
    peer_count = lax.axis_size("ctx")
    self_index = lax.axis_index("ctx")
    token_count = inputs.shape[0]
    window_len = token_count * peer_count
    block_len = token_count // BPD
    key_block = min(512, window_len)
    ends_row = jnp.cumsum(doc_lengths[0])
    owners = block_owner[0]
    input_sums = jnp.dot(
        inputs,
        lax.all_gather(basis_qkv, "ctx", axis=0, tiled=True),
        preferred_element_type=jnp.float32,
    )
    grad_sums = jnp.dot(
        out_grad,
        lax.all_gather(basis_out, "ctx", axis=0, tiled=True),
        preferred_element_type=jnp.float32,
    )
    input_proj = input_sums.astype(jnp.bfloat16)
    grad_proj = grad_sums.astype(jnp.bfloat16)
    key_all, value_all = (
        lax.all_gather(keys, "ctx", axis=0, tiled=True),
        lax.all_gather(values, "ctx", axis=0, tiled=True),
    )
    owned_mask = (owners == self_index).astype(jnp.int32)
    owned_rank = jnp.cumsum(owned_mask) - 1
    picker = (owned_mask[None, :] == 1) & (
        owned_rank[None, :] == jnp.arange(BPD, dtype=jnp.int32)[:, None]
    )
    block_numbers = jnp.arange(owners.shape[0], dtype=jnp.int32)
    owned_blocks = jnp.sum(jnp.where(picker, block_numbers[None, :], 0), axis=1)
    sources = owned_blocks // BPD
    destination = lax.dynamic_slice_in_dim(owners, self_index * BPD, BPD, 0)
    block_starts = self_index * token_count + jnp.arange(BPD, dtype=jnp.int32) * block_len
    grad_query, attn_out, key_part, value_part = attention_backward(
        queries, attn_grad, block_starts, key_all, value_all, ends_row, block_len, key_block
    )
    outgoing = slot_buffer(
        grad_query.reshape(BPD, block_len, grad_query.shape[1]), destination, peer_count
    )
    incoming = lax.all_to_all(outgoing, "ctx", split_axis=0, concat_axis=0, tiled=True)
    grad_queries = compact_slots(incoming, sources, peer_count).reshape(
        token_count, grad_query.shape[1]
    )
    query_term = jnp.einsum("tr,tc->rc", input_proj, grad_query, preferred_element_type=jnp.float32)
    out_term = jnp.einsum("tr,tc->rc", grad_proj, attn_out, preferred_element_type=jnp.float32)
    key_sums, value_sums = (
        lax.psum_scatter(key_part, "ctx", scatter_dimension=0, tiled=True),
        lax.psum_scatter(value_part, "ctx", scatter_dimension=0, tiled=True),
    )
    grad_keys = key_sums.astype(jnp.bfloat16)
    grad_values = value_sums.astype(jnp.bfloat16)
    norm_factor = 1.0 / math.sqrt(token_count * peer_count * lax.axis_size("dp"))
    qkv_term = (
        jnp.concatenate(
            [
                query_term,
                jnp.einsum("tr,tc->rc", input_proj, grad_keys, preferred_element_type=jnp.float32),
                jnp.einsum(
                    "tr,tc->rc", input_proj, grad_values, preferred_element_type=jnp.float32
                ),
            ],
            axis=1,
        )
        * norm_factor
    )
    galore_qkv, galore_out = (
        lax.psum_scatter(qkv_term, ("dp", "ctx"), scatter_dimension=0, tiled=True),
        lax.psum_scatter(out_term * norm_factor, ("dp", "ctx"), scatter_dimension=0, tiled=True),
    )
    return (grad_queries, grad_keys, grad_values, galore_qkv, galore_out)


def solution(mesh):
    in_specs = (
        P(("dp", "ctx"), None),
        P(("dp", "ctx"), None),
        P(("dp", "ctx"), None),
        P(("dp", "ctx"), None),
        P(("dp", "ctx"), None),
        P(("dp", "ctx"), None),
        P("dp", None),
        P("dp", None),
        P("ctx", None),
        P("ctx", None),
    )
    out_specs = (
        P(("dp", "ctx"), None),
        P(("dp", "ctx"), None),
        P(("dp", "ctx"), None),
        P(("dp", "ctx"), None),
        P(("dp", "ctx"), None),
    )
    return jax.shard_map(shards, mesh=mesh, in_specs=in_specs, out_specs=out_specs, check_vma=False)
```

profile of v0, /device:TPU:25, one launch (start us, length us, event | category | flops | bytes accessed | tf_op | source)
XLA Modules:
  0.0 523.9 jit_solution(10330599048275797794)
XLA Ops:
  11.4 3.3 fusion.125
  20.1 8.2 %all_gather.12 = bf16[512,128]{1,0:T(8,128)(2,1)S(1)} all-gather(bf16[128,128]{1,0:T(8,128)(2,1)S(1)} %copy-done.28), channel_id=1, replica_groups=mesh['dp'=8,'ctx'=4] {'ctx'}, dimensions={0}, use_global_device_ids=true | all-gather | bytes 163840 | tf_op jit(solution)/shard_map/all_gather | solution.py:232
  29.1 3.5 conditional.32
  29.2 1.2 select_reduce_fusion.1
  31.0 1.0 select_reduce_fusion
  32.7 8.2 %all_gather.13 = bf16[512,128]{1,0:T(8,128)(2,1)S(1)} all-gather(bf16[128,128]{1,0:T(8,128)(2,1)S(1)} %copy-done.29), channel_id=1, replica_groups=mesh['dp'=8,'ctx'=4] {'ctx'}, dimensions={0}, use_global_device_ids=true | all-gather | bytes 163840 | tf_op jit(solution)/shard_map/all_gather | solution.py:233
  40.9 1.3 log_add_fusion.3
  42.2 1.4 conditional.33
  42.2 1.3 fusion.128
  44.9 3.5 conditional.35
  45.0 1.2 select_reduce_fusion.3
  48.4 1.3 log_add_fusion.2
  49.7 1.4 conditional.36
  49.7 1.3 fusion.129
  51.7 4.1 conditional.34
  52.7 1.2 fusion.20
  54.5 1.1 convolution_add_fusion.1
  56.7 2.7 conditional.38
  59.4 1.3 log_add_fusion.1
  60.7 1.8 conditional.39
  61.3 1.1 fusion.130
  63.2 10.0 %conditional.37 = (f32[512,128]{1,0:T(8,128)S(1)}, f32[512,128]{1,0:T(8,128)S(1)}, f32[256,128]{1,0:T(8,128)}) conditional(s32[]{:T(128)} %convert_element_type.246, (f32[512,128]{1,0:T(8,128)S(1)}, f32[512,128]{1,0:T(8,128)S(1)}, f32[256,128]{1,0:T(8,128)S(1)}) %tuple.222, (s32[256]{0:T(256)}, s32[512]{0:T(512)S(1)}, s32[32,8]{1,0:T(8,128)S(1)}, ...), branch_computations={%region_23.24_spmd, %region_24.26_spmd} | conditional | flops 169541376 | bytes 4801588 | solution.py:147
  63.8 1.2 fusion.46
  65.0 1.5 slice.41
  66.4 1.5 reshape_squeeze.25
  67.9 1.1 multiply_reduce_fusion.1
  69.0 1.1 fusion.49
  70.0 1.1 convolution_add_fusion.4
  71.2 1.1 convolution_add_fusion.3
  73.8 1.5 reshape_squeeze.35
  75.3 4.8 conditional.41
  75.4 1.2 select_reduce_fusion.7
  76.6 1.2 max.11
  77.8 1.0 select_reduce_fusion.6
  78.8 1.3 multiply_add_fusion.3
  80.1 1.3 log_add_fusion
  81.4 1.4 conditional.42
  81.4 1.3 fusion.131
  83.4 9.4 %conditional.40 = (f32[512,128]{1,0:T(8,128)S(1)}, f32[512,128]{1,0:T(8,128)S(1)}, f32[256,128]{1,0:T(8,128)S(1)}) conditional(s32[]{:T(128)} %convert_element_type.249, (f32[512,128]{1,0:T(8,128)S(1)}, f32[512,128]{1,0:T(8,128)S(1)}, f32[256,128]{1,0:T(8,128)S(1)}) %tuple.226, (s32[256]{0:T(256)}, s32[512]{0:T(512)}, s32[32,8]{1,0:T(8,128)S(1)}, ...), branch_computations={%region_34.35_spmd, %region_35.37_spmd} | conditional | flops 169541376 | bytes 4793368 | solution.py:147
  84.1 1.2 fusion.72
  85.3 1.5 slice.42
  86.7 1.5 reshape_squeeze.26
  88.2 1.1 multiply_reduce_fusion.2
  89.3 1.1 fusion.75
  90.3 1.1 convolution_add_fusion.7
  91.5 1.1 convolution_add_fusion.6
  93.5 9.4 %conditional.43 = ((f32[512,128]{1,0:T(8,128)S(1)}, f32[512,128]{1,0:T(8,128)S(1)}, f32[256,128]{1,0:T(8,128)S(1)})) conditional(s32[]{:T(128)} %convert_element_type.252, (f32[512,128]{1,0:T(8,128)S(1)}, f32[512,128]{1,0:T(8,128)S(1)}, f32[256,128]{1,0:T(8,128)S(1)}) %tuple.230, (s32[256]{0:T(256)}, s32[512]{0:T(512)}, s32[32,8]{1,0:T(8,128)S(1)}, ...), branch_computations={%region_45.46_spmd, %region_46.48_spmd} | conditional | flops 169541376 | bytes 4793376 | solution.py:147
  94.1 1.2 fusion.98
  95.3 1.5 slice.43
  96.8 1.5 reshape_squeeze.27
  98.3 1.1 multiply_reduce_fusion.3
  99.3 1.1 fusion.101
  100.4 1.1 convolution_add_fusion.10
  101.5 1.1 convolution_add_fusion.9
  105.0 6.4 %convolution_multiply_fusion.12 = f32[512,1024]{1,0:T(8,128)} fusion(bf16[128,8192]{1,0:T(8,128)(2,1)S(1)} %copy-done, bf16[8192,512]{1,0:T(8,128)(2,1)} %all-gather.5.cloned.1.call-done, bf16[32,1024]{1,0:T(8,128)(2,1)S(1)} %copy-done.19, bf16[32,1024]{1,0:T(8,128)(2,1)S(1)} %copy-done.17, bf16[32,1024]{1,0:T(8,128)(2,1)S(1)} %copy-done.15, ...), kind=kOutput, calls=%fused_computation.157 | convolution fusion | flops 1209597952 | bytes 12845056 | tf_op jit(solution)/shard_map/tr,tc->rc/dot_general | solution.py:256
  113.5 16.5 %reduce-scatter.5.cloned.1.call-done = f32[128,128]{1,0:T(8,128)} async-done(((f32[512,128]{1,0:T(8,128)}), f32[128,128]{1,0:T(8,128)}) %reduce-scatter.5.cloned.1.call-update) | async-done | bytes 65552 | tf_op jit(solution)/shard_map/reduce_scatter | solution.py:258
  130.8 26.2 %reduce-scatter.7.cloned.1.call-done = f32[128,128]{1,0:T(8,128)} async-done(((f32[512,128]{1,0:T(8,128)}), f32[128,128]{1,0:T(8,128)}) %reduce-scatter.7.cloned.1.call-update) | async-done | bytes 65552 | tf_op jit(solution)/shard_map/reduce_scatter | solution.py:259
  157.9 89.0 %all-gather.3.cloned.1.call-done = bf16[8192,512]{1,0:T(8,128)(2,1)} async-done(((bf16[2048,512]{1,0:T(8,128)(2,1)}), bf16[8192,512]{1,0:T(8,128)(2,1)}) %all-gather.3.cloned.1.call-update) | async-done | bytes 8388624 | tf_op jit(solution)/shard_map/all_gather | solution.py:221
  246.9 5.3 %convolution_convert_fusion.1 = bf16[128,512]{1,0:T(8,128)(2,1)S(1)} fusion(bf16[128,8192]{1,0:T(8,128)(2,1)} %param.34, bf16[8192,512]{1,0:T(8,128)(2,1)} %all-gather.3.cloned.1.call-done), kind=kOutput, calls=%fused_computation.159 | convolution fusion | flops 1073807360 | bytes 10616832 | tf_op jit(solution)/shard_map/dot_general | solution.py:219
  253.1 1.7 maximum_multiply_fusion
  256.6 3.4 all-to-all-start
  260.4 5.9 %all-to-all-done = bf16[4,32,1024]{2,1,0:T(8,128)(2,1)S(1)} async-done(((bf16[4,32,1024]{2,1,0:T(8,128)(2,1)}), bf16[4,32,1024]{2,1,0:T(8,128)(2,1)S(1)}, u32[]{:S(2)}, u32[]{:S(2)}) %all-to-all-start) | async-done | bytes 262176 | tf_op jit(solution)/shard_map/all_to_all | solution.py:251
  267.5 112.4 %reduce-scatter.11.cloned.1.call-done = f32[16,1024]{1,0:T(8,128)} async-done(((f32[512,1024]{1,0:T(8,128)}), f32[16,1024]{1,0:T(8,128)}) %reduce-scatter.11.cloned.1.call-update) | async-done | bytes 65552 | tf_op jit(solution)/shard_map/reduce_scatter | solution.py:279
  379.9 137.2 %reduce-scatter.9.cloned.1.call-done = f32[16,1280]{1,0:T(8,128)} async-done(((f32[512,1280]{1,0:T(8,128)}), f32[16,1280]{1,0:T(8,128)}) %reduce-scatter.9.cloned.1.call-update) | async-done | bytes 81936 | tf_op jit(solution)/shard_map/reduce_scatter | solution.py:278
  (170 shorter events, 32.6 us)
Async XLA Ops:
  7.2 97.8 %copy-start = (bf16[128,8192]{1,0:T(8,128)(2,1)S(1)}, bf16[128,8192]{1,0:T(8,128)(2,1)}, u32[]{:S(2)}) copy-start(bf16[128,8192]{1,0:T(8,128)(2,1)} %param.35) | copy-start | bytes 6291460
  7.2 2.1 copy-start.34
  7.2 11.5 %copy-start.20 = (bf16[128,1024]{1,0:T(8,128)(2,1)S(1)}, bf16[128,1024]{1,0:T(8,128)(2,1)}, u32[]{:S(2)}) copy-start(bf16[128,1024]{1,0:T(8,128)(2,1)} %param.36) | copy-start | bytes 786436
  7.2 12.9 %copy-start.28 = (bf16[128,128]{1,0:T(8,128)(2,1)S(1)}, bf16[128,128]{1,0:T(8,128)(2,1)}, u32[]{:S(2)}) copy-start(bf16[128,128]{1,0:T(8,128)(2,1)} %param.37) | copy-start | bytes 98308
  7.2 25.5 %copy-start.29 = (bf16[128,128]{1,0:T(8,128)(2,1)S(1)}, bf16[128,128]{1,0:T(8,128)(2,1)}, u32[]{:S(2)}) copy-start(bf16[128,128]{1,0:T(8,128)(2,1)} %param.38) | copy-start | bytes 98308
  7.2 97.8 %all-gather.5.cloned.1.call-start = ((), (), s32[]{:S(2)}) async-start(), calls=%async_computation.9 | async-start | bytes 10485760 | tf_op jit(solution)/shard_map/all_gather | solution.py:226
  8.0 122.0 %reduce-scatter.5.cloned.1.call-start = ((), (), s32[]{:S(2)}) async-start(), calls=%async_computation.5 | async-start | bytes 327680 | tf_op jit(solution)/shard_map/reduce_scatter | solution.py:258
  17.8 42.9 %copy-start.10 = (s32[32,8]{1,0:T(8,128)}, s32[32,8]{1,0:T(8,128)S(1)}, u32[]{:S(2)}) copy-start(s32[32,8]{1,0:T(8,128)S(1)} %broadcast_in_dim.155) | copy-start | bytes 3076
  20.1 36.6 %copy-start.22 = (f32[256]{0:T(256)}, f32[256]{0:T(256)S(1)}, u32[]{:S(2)}) copy-start(f32[256]{0:T(256)S(1)} %broadcast.216) | copy-start | bytes 3076
  20.1 36.6 %copy-start.25 = (f32[256]{0:T(256)}, f32[256]{0:T(256)S(1)}, u32[]{:S(2)}) copy-start(f32[256]{0:T(256)S(1)} %broadcast.217) | copy-start | bytes 3076
  28.4 34.0 %copy-start.26 = (s32[512]{0:T(512)}, s32[512]{0:T(512)S(1)}, u32[]{:S(2)}) copy-start(s32[512]{0:T(512)S(1)} %convert_reduce_fusion) | copy-start | bytes 6148
  29.1 20.5 %copy-start.32 = (s32[256]{0:T(256)}, s32[256]{0:T(256)S(1)}, u32[]{:S(2)}) copy-start(s32[256]{0:T(256)S(1)} %get-tuple-element.1200) | copy-start | bytes 3076
  43.6 8.2 %copy-start.12 = (bf16[32,1024]{1,0:T(8,128)(2,1)}, bf16[32,1024]{1,0:T(8,128)(2,1)S(1)}, u32[]{:S(2)}) copy-start(bf16[32,1024]{1,0:T(8,128)(2,1)S(1)} %get-tuple-element.1152) | copy-start | bytes 196612
  51.1 0.7 copy-start.3
  51.1 0.7 copy-start.14
  51.1 5.6 %copy-start.30 = (s32[256]{0:T(256)S(1)}, s32[256]{0:T(256)}, u32[]{:S(2)}) copy-start(s32[256]{0:T(256)} %get-tuple-element.1199) | copy-start | bytes 3076
  55.9 6.6 %copy-start.6 = (f32[256,128]{1,0:T(8,128)}, f32[256,128]{1,0:T(8,128)S(1)}, u32[]{:S(2)}) copy-start(f32[256,128]{1,0:T(8,128)S(1)} %get-tuple-element.1131) | copy-start | bytes 393220
  56.6 4.0 copy-start.21
  60.7 0.6 copy-start.31
  62.5 0.7 copy-start.4
  62.5 0.7 copy-start.16
  63.2 0.6 copy-start.27
  73.2 8.2 %copy-start.11 = (s32[32,8]{1,0:T(8,128)S(1)}, s32[32,8]{1,0:T(8,128)}, u32[]{:S(2)}) copy-start(s32[32,8]{1,0:T(8,128)} %copy-done.10) | copy-start | bytes 3076
  82.8 0.7 copy-start.5
  82.8 0.7 copy-start.18
  92.8 0.6 copy-start.8
  102.9 0.7 copy-start.1
  102.9 0.8 copy-start.2
  102.9 2.1 copy-start.13
  102.9 2.1 copy-start.15
  102.9 2.1 copy-start.17
  102.9 2.1 copy-start.19
  103.6 53.5 %reduce-scatter.7.cloned.1.call-start = ((), (), s32[]{:S(2)}) async-start(), calls=%async_computation.6 | async-start | bytes 327680 | tf_op jit(solution)/shard_map/reduce_scatter | solution.py:259
  104.3 142.6 %all-gather.3.cloned.1.call-start = ((), (), s32[]{:S(2)}) async-start(), calls=%async_computation.7 | async-start | bytes 10485760 | tf_op jit(solution)/shard_map/all_gather | solution.py:221
  104.9 274.9 %reduce-scatter.11.cloned.1.call-start = ((), (), s32[]{:S(2)}) async-start(), calls=%async_computation.10 | async-start | bytes 2162688 | tf_op jit(solution)/shard_map/reduce_scatter | solution.py:279
  111.5 0.9 copy-start.7
  111.5 1.9 copy-start.9
  111.5 405.5 %reduce-scatter.9.cloned.1.call-start = ((), (), s32[]{:S(2)}) async-start(), calls=%async_computation.8 | async-start | bytes 2703360 | tf_op jit(solution)/shard_map/reduce_scatter | solution.py:278
  130.8 121.6 %copy-start.23 = (bf16[128,128]{1,0:T(8,128)(2,1)}, bf16[128,128]{1,0:T(8,128)(2,1)S(1)}, u32[]{:S(2)}) copy-start(bf16[128,128]{1,0:T(8,128)(2,1)S(1)} %convert_element_type.255) | copy-start | bytes 98308
  157.9 94.3 %copy-start.24 = (bf16[128,128]{1,0:T(8,128)(2,1)}, bf16[128,128]{1,0:T(8,128)(2,1)S(1)}, u32[]{:S(2)}) copy-start(bf16[128,128]{1,0:T(8,128)(2,1)S(1)} %convert_element_type.256) | copy-start | bytes 98308
  254.8 0.7 copy-start.33
  256.6 9.7 %all-to-all-start = ((bf16[4,32,1024]{2,1,0:T(8,128)(2,1)}), bf16[4,32,1024]{2,1,0:T(8,128)(2,1)S(1)}, u32[]{:S(2)}, u32[]{:S(2)}) async-start(bf16[4,32,1024]{2,1,0:T(8,128)(2,1)} %copy.37), calls=%async_computation | async-start | bytes 524288 | tf_op jit(solution)/shard_map/all_to_all | solution.py:251
Sparse Core Ops, SparseCore 0:
  9.9 90.6 all-gather.4
  104.0 25.9 reduce-scatter.4
  133.0 24.0 reduce-scatter.6
  158.8 88.0 all-gather.2
  249.6 130.2 reduce-scatter.10
  382.7 134.3 reduce-scatter.8
where the time goes:
time: 535 us; the launch traced here: 524 us
  waiting for transfers between devices  389 us (73%)
  matrix products  39.8 us (7%)
  other arithmetic  30.2 us (6%)
  local copies, waits for them, and re-layouts  24.3 us (5%)
  between operations  20 us (4%)
  blocking collectives  16.5 us (3%)
    reduce_scatter x1, waiting for transfers between devices, shards(): lax.psum_scatter(qkv_term, ('dp', 'ctx'), scatter_dimension=0, tiled=True)  137 us
    reduce_scatter x1, waiting for transfers between devices, shards(): lax.psum_scatter(out_term * norm_factor, ('dp', 'ctx'), scatter_dimension...  112 us
    all_gather x1, waiting for transfers between devices, shards(): lax.all_gather(basis_qkv, 'ctx', axis=0, tiled=True)  89 us
    reduce_scatter x1, waiting for transfers between devices, shards(): lax.psum_scatter(value_part, 'ctx', scatter_dimension=0, tiled=True)  26.2 us
    reduce_scatter x1, waiting for transfers between devices, shards(): lax.psum_scatter(key_part, 'ctx', scatter_dimension=0, tiled=True)  16.5 us
  transfers between devices with their start and end apart: 7, of which 6 were waited for; matrix products, arithmetic and copies ran while one was open for 17% of the time, Pallas kernels for 0%

commit v1 on v0

--- a/solution.py
+++ b/solution.py
@@ -1,8 +1,11 @@
+import functools
 import math
 
 import jax
 import jax.numpy as jnp
 from jax import lax
+from jax.experimental import pallas as pl
+from jax.experimental.pallas import tpu as pltpu
 from jax.sharding import PartitionSpec as P
 
 HD = 128
@@ -281,6 +284,408 @@
     return (grad_queries, grad_keys, grad_values, galore_qkv, galore_out)
 
 
+MESH = pl.DeviceIdType.MESH
+CHUNKS = 4
+
+
+def fused_kernel(
+    dp_size,
+    scale_out,
+    lengths_ref,
+    owner_ref,
+    x_hbm,
+    g_hbm,
+    bq_hbm,
+    bo_hbm,
+    q_ref,
+    k_ref,
+    v_ref,
+    do_ref,
+    gq_out,
+    gk_out,
+    gv_out,
+    gqkv_out,
+    gout_out,
+    xbuf,
+    bbuf,
+    kbuf,
+    vbuf,
+    bias,
+    dkv,
+    dkv_in,
+    act,
+    act_in,
+    slots,
+    gq_in,
+    acc,
+    tbuf,
+    r1,
+    s1,
+    r2,
+    fin,
+    fin_in,
+    lsem,
+    kv_s,
+    kv_r,
+    x_s,
+    x_r,
+    b_s,
+    b_r,
+    dkv_s,
+    dkv_r,
+    gq_s,
+    gq_r,
+    act_s,
+    act_r,
+    t_s,
+    t_r,
+    z_s,
+    z_r,
+    f_s,
+    f_r,
+):
+    dp = lax.axis_index("dp")
+    me = lax.axis_index("ctx")
+    core = lax.rem(dp, 2)
+    z = dp // 2
+    nz = dp_size // 2
+    sib = dp + 1 - 2 * core
+    peers = (me, me + 1 - 2 * lax.rem(me, 2), lax.rem(me + 2, 4), 3 - me)
+    zpeers = [lax.rem(z + k, nz) for k in range(nz)]
+    tokens = q_ref.shape[0]
+    window = 4 * tokens
+    depth = bq_hbm.shape[0]
+    step = depth // CHUNKS
+    blk = tokens // BPD
+    f32, bf16 = jnp.float32, jnp.bfloat16
+
+    def remote(src, dst, send, recv, dev):
+        return pltpu.make_async_remote_copy(
+            src_ref=src, dst_ref=dst, send_sem=send, recv_sem=recv, device_id=dev, device_id_type=MESH
+        )
+
+    own_x0 = pltpu.make_async_copy(x_hbm, xbuf.at[0], lsem.at[0])
+    own_x1 = pltpu.make_async_copy(g_hbm, xbuf.at[0], lsem.at[0])
+    own_b0 = pltpu.make_async_copy(bq_hbm, bbuf.at[0], lsem.at[1])
+    own_b1 = pltpu.make_async_copy(bo_hbm, bbuf.at[0], lsem.at[1])
+
+    @pl.when(core == 0)
+    def _():
+        own_b0.start()
+        own_x0.start()
+
+    @pl.when(core == 1)
+    def _():
+        own_b1.start()
+        own_x1.start()
+
+    barrier = pltpu.get_barrier_semaphore()
+    for r in (1, 2, 3):
+        pl.semaphore_signal(barrier, inc=1, device_id=(dp, peers[r]), device_id_type=MESH)
+    pl.semaphore_signal(barrier, inc=1, device_id=(sib, me), device_id_type=MESH)
+    for k in range(1, nz):
+        pl.semaphore_signal(
+            barrier, inc=1, device_id=(2 * zpeers[k] + core, me), device_id_type=MESH
+        )
+    pl.semaphore_wait(barrier, 3 + 1 + nz - 1)
+
+    kv_copies = []
+    for r in (1, 2, 3):
+        for i, (src, dst) in enumerate(((k_ref, kbuf), (v_ref, vbuf))):
+            n = 2 * (r - 1) + i
+            kv_copies.append(
+                remote(src, dst.at[me], kv_s.at[n], kv_r.at[n], (dp, peers[r]))
+            )
+    for c in kv_copies:
+        c.start()
+
+    own_b0.wait()
+
+    def rows(chunk):
+        return pl.ds(chunk * step, step)
+
+    def basis_copy(slot, chunk, to, via, n):
+        m = (to - 1) * CHUNKS + chunk
+        return remote(
+            bbuf.at[slot, rows(chunk)], bbuf.at[to, rows(chunk)], b_s.at[n], b_r.at[m], (dp, peers[via])
+        )
+
+    half = CHUNKS // 2
+    to_x = [basis_copy(0, c, 1, 1, c) for c in range(CHUNKS)]
+    to_y = [basis_copy(0, c, 2, 2, CHUNKS + c) for c in range(CHUNKS)]
+    fwd = [
+        basis_copy(1, c, 3, 2, 2 * CHUNKS + c)
+        if c < half
+        else basis_copy(2, c, 3, 1, 2 * CHUNKS + c)
+        for c in range(CHUNKS)
+    ]
+    for i in range(CHUNKS):
+        to_x[i].start()
+        to_y[(i + half) % CHUNKS].start()
+
+    sib_x0 = remote(g_hbm, xbuf.at[1], x_s, x_r, (sib, me))
+    sib_x1 = remote(x_hbm, xbuf.at[1], x_s, x_r, (sib, me))
+
+    @pl.when(core == 0)
+    def _():
+        sib_x0.start()
+
+    @pl.when(core == 1)
+    def _():
+        sib_x1.start()
+
+    kbuf[me] = k_ref[...]
+    vbuf[me] = v_ref[...]
+    pos = me * tokens + lax.broadcasted_iota(jnp.int32, (tokens, 1), 0)
+    begin = jnp.zeros((tokens, 1), jnp.int32)
+    end = jnp.int32(0)
+    for n in range(lengths_ref.shape[1]):
+        end = end + lengths_ref[0, n]
+        begin = jnp.where(pos >= end, end, begin)
+    key_pos = lax.broadcasted_iota(jnp.int32, (tokens, window), 1)
+    bias[...] = jnp.where((key_pos <= pos) & (key_pos >= begin), 0.0, NEG_LARGE).astype(f32)
+    dkv[...] = jnp.zeros_like(dkv)
+    act[...] = jnp.zeros_like(act)
+
+    for c in kv_copies:
+        c.wait()
+
+    scale = HD ** (-0.5)
+    across = (((1,), (1,)), ((), ()))
+    down = (((0,), (0,)), ((), ()))
+
+    def head(h, carry):
+        cols = pl.ds(pl.multiple_of(h * HD, HD), HD)
+        key = kbuf[...].reshape(window, HD)
+        val = vbuf[...].reshape(window, HD)
+        q = q_ref[:, cols]
+        do = do_ref[:, cols]
+        s = lax.dot_general(q, key, across, preferred_element_type=f32) * scale + bias[...]
+        top = jnp.max(s, axis=1, keepdims=True)
+        e = jnp.exp(s - top)
+        p = e * (1.0 / jnp.sum(e, axis=1, keepdims=True))
+        w = p.astype(bf16)
+        o = jnp.dot(w, val, preferred_element_type=f32).astype(bf16)
+        delta = jnp.sum(do.astype(f32) * o.astype(f32), axis=1, keepdims=True)
+        dprob = lax.dot_general(do, val, across, preferred_element_type=f32)
+        ds = (p * (dprob - delta) * scale).astype(bf16)
+        act[0, :, cols] = jnp.dot(ds, key, preferred_element_type=f32).astype(bf16)
+        act[1, :, cols] = o
+        dk = lax.dot_general(ds, q, down, preferred_element_type=f32)
+        dv = lax.dot_general(w, do, down, preferred_element_type=f32)
+        dkv[0] += dk.reshape(4, tokens, HD)
+        dkv[1] += dv.reshape(4, tokens, HD)
+        return carry
+
+    lax.fori_loop(0, HQ, head, 0)
+
+    dkv_copies = [
+        remote(dkv.at[:, peers[r]], dkv_in.at[r - 1], dkv_s.at[r - 1], dkv_r.at[r - 1], (dp, peers[r]))
+        for r in (1, 2, 3)
+    ]
+    for c in dkv_copies:
+        c.start()
+
+    wide = HQ * HD
+    for d in range(4):
+        chosen = jnp.zeros((blk, wide), f32)
+        for j in range(BPD):
+            piece = act[0, j * blk : (j + 1) * blk, :wide].astype(f32)
+            chosen = jnp.where(owner_ref[0, me * BPD + j] == d, piece, chosen)
+        slots[d] = chosen.astype(bf16)
+    gq_copies = [
+        remote(slots.at[peers[r]], gq_in.at[me], gq_s.at[r - 1], gq_r.at[r - 1], (dp, peers[r]))
+        for r in (1, 2, 3)
+    ]
+    for c in gq_copies:
+        c.start()
+    gq_in[me] = slots[me]
+
+    for c in dkv_copies:
+        c.wait()
+    for i, out in enumerate((gk_out, gv_out)):
+        total = dkv[i, me] + dkv_in[0, i] + dkv_in[1, i] + dkv_in[2, i]
+        total = total.astype(bf16)
+        out[...] = total
+        act[0, :, wide + i * HD : wide + (i + 1) * HD] = total
+    act_copy = remote(act.at[1 - core], act_in, act_s, act_r, (sib, me))
+    act_copy.start()
+
+    own_x0.wait()
+    sib_x0.wait()
+
+    def add(slot, chunk, first=False):
+        at = pl.multiple_of(peers[slot] * depth + chunk * step, step)
+        x = xbuf[:, :, pl.ds(at, step)].reshape(2 * tokens, step)
+        part = jnp.dot(x, bbuf[slot, chunk * step : (chunk + 1) * step, :], preferred_element_type=f32)
+        if first:
+            acc[...] = part
+        else:
+            acc[...] += part
+
+    for c in range(CHUNKS):
+        add(0, c, c == 0)
+    for i in range(CHUNKS):
+        j = (i + half) % CHUNKS
+        to_x[i].wait_recv()
+        if i < half:
+            fwd[i].start()
+        to_y[j].wait_recv()
+        if j >= half:
+            fwd[j].start()
+        add(1, i)
+        add(2, j)
+    act_copy.wait()
+    for c in gq_copies:
+        c.wait()
+    for d in range(4):
+        gq_out[d * blk : (d + 1) * blk, :] = gq_in[d]
+    for i in range(half):
+        fwd[i].wait_recv()
+        add(3, i)
+        fwd[i + half].wait_recv()
+        add(3, i + half)
+
+    own_rows = acc.shape[1] // (dp_size * 4)
+    per_dp = 4 * own_rows
+    for d in range(dp_size):
+        left = acc[:, (d // 2) * 2 * per_dp : (d // 2 + 1) * 2 * per_dp].astype(bf16)
+        if d % 2 == 0:
+            both = lax.dot_general(
+                left[:tokens], act[core], down, preferred_element_type=f32
+            ) + lax.dot_general(left[tokens:], act_in[...], down, preferred_element_type=f32)
+            tbuf[d : d + 2] = both.astype(bf16).reshape(2, 4, own_rows, both.shape[1])
+    t_copies = [
+        remote(tbuf.at[:, peers[r]], r1.at[r - 1], t_s.at[r - 1], t_r.at[r - 1], (dp, peers[r]))
+        for r in (1, 2, 3)
+    ]
+    for r in (2, 0, 1):
+        t_copies[r].start()
+    for c in to_x + to_y + fwd:
+        c.wait_send()
+    for c in t_copies:
+        c.wait()
+    for d in range(dp_size):
+        total = tbuf[d, me].astype(f32) + r1[0, d].astype(f32)
+        total = total + (r1[1, d].astype(f32) + r1[2, d].astype(f32))
+        s1[d // 2, d % 2] = total.astype(bf16)
+    z_copies = [
+        remote(
+            s1.at[zpeers[k]], r2.at[k - 1], z_s.at[k - 1], z_r.at[k - 1], (2 * zpeers[k] + core, me)
+        )
+        for k in range(1, nz)
+    ]
+    for c in z_copies:
+        c.start()
+    for c in z_copies:
+        c.wait()
+    total = s1[z].astype(f32)
+    for k in range(1, nz):
+        total = total + r2[k - 1].astype(f32)
+    fin[...] = total * scale_out
+    f_copy = remote(fin.at[1 - core], fin_in, f_s, f_r, (sib, me))
+    f_copy.start()
+    f_copy.wait()
+    mine = fin[core]
+    other = fin_in[...]
+    gqkv_out[...] = jnp.where(core == 0, mine, other)
+    gout_out[...] = jnp.where(core == 0, other, mine)[:, :wide]
+
+
+def fused_shards(
+    inputs,
+    out_grad,
+    queries,
+    keys,
+    values,
+    attn_grad,
+    doc_lengths,
+    block_owner,
+    basis_qkv,
+    basis_out,
+):
+    dp_size = lax.axis_size("dp")
+    nz = dp_size // 2
+    tokens, width = inputs.shape
+    depth, rank = basis_qkv.shape
+    wide = queries.shape[1]
+    cols = wide + 2 * HD
+    own_rows = rank // (dp_size * 4)
+    blk = tokens // BPD
+    f32, bf16 = jnp.float32, jnp.bfloat16
+    norm_factor = 1.0 / math.sqrt(tokens * 4 * dp_size)
+    vmem = pl.BlockSpec(memory_space=pltpu.VMEM)
+    smem = pl.BlockSpec(memory_space=pltpu.SMEM)
+    hbm = pl.BlockSpec(memory_space=pl.ANY)
+    dma = pltpu.SemaphoreType.DMA
+    return pl.pallas_call(
+        functools.partial(fused_kernel, dp_size, norm_factor),
+        out_shape=(
+            jax.ShapeDtypeStruct((tokens, wide), bf16),
+            jax.ShapeDtypeStruct((tokens, HD), bf16),
+            jax.ShapeDtypeStruct((tokens, HD), bf16),
+            jax.ShapeDtypeStruct((own_rows, cols), f32),
+            jax.ShapeDtypeStruct((own_rows, wide), f32),
+        ),
+        in_specs=[smem, smem, hbm, hbm, hbm, hbm, vmem, vmem, vmem, vmem],
+        out_specs=[vmem] * 5,
+        scratch_shapes=[
+            pltpu.VMEM((2, tokens, width), bf16),
+            pltpu.VMEM((4, depth, rank), bf16),
+            pltpu.VMEM((4, tokens, HD), bf16),
+            pltpu.VMEM((4, tokens, HD), bf16),
+            pltpu.VMEM((tokens, 4 * tokens), f32),
+            pltpu.VMEM((2, 4, tokens, HD), f32),
+            pltpu.VMEM((3, 2, tokens, HD), f32),
+            pltpu.VMEM((2, tokens, cols), bf16),
+            pltpu.VMEM((tokens, cols), bf16),
+            pltpu.VMEM((4, blk, wide), bf16),
+            pltpu.VMEM((4, blk, wide), bf16),
+            pltpu.VMEM((2 * tokens, rank), f32),
+            pltpu.VMEM((dp_size, 4, own_rows, cols), bf16),
+            pltpu.VMEM((3, dp_size, own_rows, cols), bf16),
+            pltpu.VMEM((nz, 2, own_rows, cols), bf16),
+            pltpu.VMEM((nz - 1, 2, own_rows, cols), bf16),
+            pltpu.VMEM((2, own_rows, cols), f32),
+            pltpu.VMEM((own_rows, cols), f32),
+            dma((2,)),
+            dma((6,)),
+            dma((6,)),
+            dma,
+            dma,
+            dma((3 * CHUNKS,)),
+            dma((3 * CHUNKS,)),
+            dma((3,)),
+            dma((3,)),
+            dma((3,)),
+            dma((3,)),
+            dma,
+            dma,
+            dma((3,)),
+            dma((3,)),
+            dma((nz - 1,)),
+            dma((nz - 1,)),
+            dma,
+            dma,
+        ],
+        compiler_params=pltpu.CompilerParams(
+            collective_id=0, has_side_effects=True, vmem_limit_bytes=48 * 1024 * 1024
+        ),
+        name="fused",
+    )(
+        doc_lengths,
+        block_owner,
+        inputs,
+        out_grad,
+        basis_qkv,
+        basis_out,
+        queries,
+        keys,
+        values,
+        attn_grad,
+    )
+
+
 def solution(mesh):
     in_specs = (
         P(("dp", "ctx"), None),
@@ -301,4 +706,5 @@
         P(("dp", "ctx"), None),
         P(("dp", "ctx"), None),
     )
-    return jax.shard_map(shards, mesh=mesh, in_specs=in_specs, out_specs=out_specs, check_vma=False)
+    body = fused_shards if mesh.shape["ctx"] == 4 and mesh.shape["dp"] == 8 else shards
+    return jax.shard_map(body, mesh=mesh, in_specs=in_specs, out_specs=out_specs, check_vma=False)

time: 535 us -> 124 us (0.23); the launches traced: 524 us -> 122 us
  waiting for transfers between devices: 389 us -> 0 us
  Pallas kernels: 0 us -> 110 us
  matrix products: 39.8 us -> 0 us
  other arithmetic: 30.2 us -> 0 us
  between operations: 20 us -> 0.66 us
  blocking collectives: 16.5 us -> 0 us
  local copies, waits for them, and re-layouts: 24.3 us -> 11.1 us
    reduce_scatter x4 -> x0, waiting for transfers between devices: 292 us -> none  [the longest x1 137 us: shards(): lax.psum_scatter(qkv_term, ('dp', 'ctx'), scatter_dimension=0, tiled=True)]
    pallas_call x0 -> x1, Pallas kernels: none -> 110 us  [fused_shards(): pl.pallas_call(functools.partial(fused_kernel, dp_size, norm_factor), out...]
    all_gather x2 -> x0, waiting for transfers between devices: 89 us -> none  [the longest x1 89 us: shards(): lax.all_gather(basis_qkv, 'ctx', axis=0, tiled=True)]
    dot_general x35 -> x0, matrix products: 39.8 us -> none  [the longest x8 8.5 us: block_scores(): lax.dot_general(query_rows, key_piece, across, preferred_element_type=jnp...]
    all_gather x2 -> x0, blocking collectives: 16.5 us -> none  [the longest x1 8.24 us: shards(): lax.all_gather(keys, 'ctx', axis=0, tiled=True)]
    add x13 -> x0, other arithmetic: 11.1 us -> none  [the longest x4 5.1 us: attend_group(): log_total = peak_score + jnp.log(denom_total)]
    reduce_sum x11 -> x0, other arithmetic: 8.11 us -> none  [the longest x4 3.93 us: stats_compute(): jnp.sum(shifted, axis=1)]
    another operation x15 -> x0, local copies, waits for them, and re-layouts: 7.94 us -> none  [the longest x4 4.49 us: attention_backward(): dout_view[lower_row:lower_row + block_len, 0].reshape(block_len * HQ, HD)]
  transfers between devices with their start and end apart: 7 -> 0, of which waited for: 6 -> 0; matrix products, arithmetic and copies ran while one was open for 17% -> 0% of each run, Pallas kernels for 0% -> 0%
where the time goes in v1:
time: 124 us; the launch traced here: 122 us
  Pallas kernels  110 us (89%)
  local copies, waits for them, and re-layouts  11.1 us (9%)
    pallas_call x1, Pallas kernels, fused_shards(): pl.pallas_call(functools.partial(fused_kernel, dp_size, norm_factor), out...  110 us
    unnamed x21, local copies, waits for them, and re-layouts  11.1 us

profile of v1, /device:TPU:25, one launch (start us, length us, event | category | flops | bytes accessed | tf_op | source)
XLA Modules:
  0.0 121.8 jit_solution(8640909251046559378)
XLA Ops:
  0.6 0.0 copy-start
  0.6 1.6 %copy-done = bf16[128,8192]{1,0:T(8,128)(2,1)S(1)} copy-done((bf16[128,8192]{1,0:T(8,128)(2,1)S(1)}, bf16[128,8192]{1,0:T(8,128)(2,1)}, u32[]{:S(2)}) %copy-start) | copy-done | bytes 2097176
  2.2 0.0 copy-start.1
  2.2 1.6 %copy-done.1 = bf16[128,8192]{1,0:T(8,128)(2,1)S(1)} copy-done((bf16[128,8192]{1,0:T(8,128)(2,1)S(1)}, bf16[128,8192]{1,0:T(8,128)(2,1)}, u32[]{:S(2)}) %copy-start.1) | copy-done | bytes 2097176
  3.8 0.0 copy-start.2
  3.8 0.9 copy-done.2
  4.8 0.0 copy-start.3
  4.8 0.9 copy-done.3
  5.7 0.0 copy-start.4
  5.7 0.8 copy-done.4
  6.5 0.0 copy-start.5
  6.5 0.8 copy-done.5
  7.2 0.0 copy-start.6
  7.2 0.7 copy-done.6
  7.9 0.0 copy-start.7
  7.9 0.7 copy-done.7
  8.5 110.1 %fused.1 = (bf16[128,1024]{1,0:T(8,128)(2,1)S(1)}, bf16[128,128]{1,0:T(8,128)(2,1)S(1)}, bf16[128,128]{1,0:T(8,128)(2,1)S(1)}, f32[16,1280]{1,0:T(8,128)S(1)}, f32[16,1024]{1,0:T(8,128)S(1)}) custom-call(s32[1,12]{1,0:T(1,128)S(1)} %copy-done.6, s32[1,16]{1,0:T(1,128)S(1)} %copy-done.7, bf16[128,8192]{1,0:T(8,128)(2,1)S(1)} %copy-done, ...), custom_call_target="tpu_custom_call" | custom-call | tf_op jit(solution)/shard_map/fused/pallas_call | solution.py:621
  118.6 0.7 copy.20
  119.3 0.6 copy.21
  120.0 0.6 copy.22
  120.6 0.6 copy.23
  121.2 0.6 copy.24
Async XLA Ops:
  0.6 1.6 %copy-start = (bf16[128,8192]{1,0:T(8,128)(2,1)S(1)}, bf16[128,8192]{1,0:T(8,128)(2,1)}, u32[]{:S(2)}) copy-start(bf16[128,8192]{1,0:T(8,128)(2,1)} %x_hbm.1) | copy-start | bytes 6291460
  2.2 1.6 %copy-start.1 = (bf16[128,8192]{1,0:T(8,128)(2,1)S(1)}, bf16[128,8192]{1,0:T(8,128)(2,1)}, u32[]{:S(2)}) copy-start(bf16[128,8192]{1,0:T(8,128)(2,1)} %g_hbm.1) | copy-start | bytes 6291460
  3.8 0.9 copy-start.2
  4.8 0.9 copy-start.3
  5.7 0.8 copy-start.4
  6.5 0.8 copy-start.5
  7.2 0.7 copy-start.6
  7.9 0.7 copy-start.7

commit v2 on v1

--- a/solution.py
+++ b/solution.py
@@ -285,27 +285,31 @@
 
 
 MESH = pl.DeviceIdType.MESH
-CHUNKS = 4
+CHUNKS = 8
 
 
 def fused_kernel(
     dp_size,
     scale_out,
-    lengths_ref,
-    owner_ref,
+    lengths_hbm,
+    owner_hbm,
     x_hbm,
     g_hbm,
     bq_hbm,
     bo_hbm,
-    q_ref,
-    k_ref,
-    v_ref,
-    do_ref,
+    q_hbm,
+    k_hbm,
+    v_hbm,
+    do_hbm,
     gq_out,
     gk_out,
     gv_out,
     gqkv_out,
     gout_out,
+    lengths_ref,
+    owner_ref,
+    q_ref,
+    do_ref,
     xbuf,
     bbuf,
     kbuf,
@@ -379,10 +383,26 @@
         own_b1.start()
         own_x1.start()
 
+    small = [
+        pltpu.make_async_copy(src, dst, lsem.at[2 + n])
+        for n, (src, dst) in enumerate(
+            (
+                (lengths_hbm, lengths_ref),
+                (owner_hbm, owner_ref),
+                (q_hbm, q_ref),
+                (do_hbm, do_ref),
+                (k_hbm, kbuf.at[me]),
+                (v_hbm, vbuf.at[me]),
+            )
+        )
+    ]
+    for c in small:
+        c.start()
     barrier = pltpu.get_barrier_semaphore()
     for r in (1, 2, 3):
         pl.semaphore_signal(barrier, inc=1, device_id=(dp, peers[r]), device_id_type=MESH)
     pl.semaphore_signal(barrier, inc=1, device_id=(sib, me), device_id_type=MESH)
+    zp = 2 * (z + 1 - 2 * lax.rem(z, 2)) + core
     for k in range(1, nz):
         pl.semaphore_signal(
             barrier, inc=1, device_id=(2 * zpeers[k] + core, me), device_id_type=MESH
@@ -391,7 +411,7 @@
 
     kv_copies = []
     for r in (1, 2, 3):
-        for i, (src, dst) in enumerate(((k_ref, kbuf), (v_ref, vbuf))):
+        for i, (src, dst) in enumerate(((k_hbm, kbuf), (v_hbm, vbuf))):
             n = 2 * (r - 1) + i
             kv_copies.append(
                 remote(src, dst.at[me], kv_s.at[n], kv_r.at[n], (dp, peers[r]))
@@ -401,27 +421,47 @@
 
     own_b0.wait()
 
-    def rows(chunk):
-        return pl.ds(chunk * step, step)
-
-    def basis_copy(slot, chunk, to, via, n):
-        m = (to - 1) * CHUNKS + chunk
+    par = lax.rem(z, 2)
+
+    def spot(k):
+        return k + par * (CHUNKS - 1 - 2 * k)
+
+    def rows(k):
+        return pl.ds(pl.multiple_of(spot(k) * step, step), step)
+
+    unit = CHUNKS // 4
+    count = [0]
+
+    def basis_copy(slot, k, to, dev):
+        n = count[0]
+        count[0] += 1
+        m = (to - 1) * CHUNKS + spot(k)
         return remote(
-            bbuf.at[slot, rows(chunk)], bbuf.at[to, rows(chunk)], b_s.at[n], b_r.at[m], (dp, peers[via])
-        )
-
-    half = CHUNKS // 2
-    to_x = [basis_copy(0, c, 1, 1, c) for c in range(CHUNKS)]
-    to_y = [basis_copy(0, c, 2, 2, CHUNKS + c) for c in range(CHUNKS)]
-    fwd = [
-        basis_copy(1, c, 3, 2, 2 * CHUNKS + c)
-        if c < half
-        else basis_copy(2, c, 3, 1, 2 * CHUNKS + c)
-        for c in range(CHUNKS)
-    ]
-    for i in range(CHUNKS):
-        to_x[i].start()
-        to_y[(i + half) % CHUNKS].start()
+            bbuf.at[slot, rows(k)], bbuf.at[to, rows(k)], b_s.at[n], b_r.at[m], dev
+        )
+
+    def arrived(slot, k):
+        m = (slot - 1) * CHUNKS + spot(k)
+        remote(
+            bbuf.at[0, rows(k)], bbuf.at[slot, rows(k)], b_s.at[0], b_r.at[m], x_dev
+        ).wait_recv()
+
+    x_dev, y_dev, z_dev = (dp, peers[1]), (dp, peers[2]), (zp, me)
+    groups = [list(range(g * unit, (g + 1) * unit)) for g in range(4)]
+    early, late = [], []
+    for k, j in zip(groups[0], groups[1]):
+        early.append(basis_copy(0, k, 1, x_dev))
+        early.append(basis_copy(0, j, 2, y_dev))
+    for k, j in zip(groups[1] + groups[2], groups[0] + groups[3]):
+        late.append(basis_copy(0, k, 1, x_dev))
+        late.append(basis_copy(0, j, 2, y_dev))
+    fwd_y = [basis_copy(1, k, 3, y_dev) for k in groups[0]]
+    fwd_x = [basis_copy(2, k, 3, x_dev) for k in groups[1]]
+    over_z1 = [basis_copy(1, k, 1, z_dev) for k in groups[0]]
+    over_z2 = [basis_copy(2, k, 2, z_dev) for k in groups[1]]
+    over_z3 = [basis_copy(3, k, 3, z_dev) for k in groups[0] + groups[1]]
+    for c in early:
+        c.start()
 
     sib_x0 = remote(g_hbm, xbuf.at[1], x_s, x_r, (sib, me))
     sib_x1 = remote(x_hbm, xbuf.at[1], x_s, x_r, (sib, me))
@@ -434,8 +474,8 @@
     def _():
         sib_x1.start()
 
-    kbuf[me] = k_ref[...]
-    vbuf[me] = v_ref[...]
+    for c in small:
+        c.wait()
     pos = me * tokens + lax.broadcasted_iota(jnp.int32, (tokens, 1), 0)
     begin = jnp.zeros((tokens, 1), jnp.int32)
     end = jnp.int32(0)
@@ -479,6 +519,14 @@
 
     lax.fori_loop(0, HQ, head, 0)
 
+    for i in range(unit):
+        arrived(1, groups[0][i])
+        fwd_y[i].start()
+        over_z1[i].start()
+        arrived(2, groups[1][i])
+        fwd_x[i].start()
+        over_z2[i].start()
+
     dkv_copies = [
         remote(dkv.at[:, peers[r]], dkv_in.at[r - 1], dkv_s.at[r - 1], dkv_r.at[r - 1], (dp, peers[r]))
         for r in (1, 2, 3)
@@ -514,37 +562,52 @@
     own_x0.wait()
     sib_x0.wait()
 
-    def add(slot, chunk, first=False):
-        at = pl.multiple_of(peers[slot] * depth + chunk * step, step)
+    def add(slot, k, first=False):
+        at = pl.multiple_of(peers[slot] * depth + spot(k) * step, step)
         x = xbuf[:, :, pl.ds(at, step)].reshape(2 * tokens, step)
-        part = jnp.dot(x, bbuf[slot, chunk * step : (chunk + 1) * step, :], preferred_element_type=f32)
+        part = jnp.dot(x, bbuf[slot, rows(k), :], preferred_element_type=f32)
         if first:
             acc[...] = part
         else:
             acc[...] += part
 
-    for c in range(CHUNKS):
-        add(0, c, c == 0)
-    for i in range(CHUNKS):
-        j = (i + half) % CHUNKS
-        to_x[i].wait_recv()
-        if i < half:
-            fwd[i].start()
-        to_y[j].wait_recv()
-        if j >= half:
-            fwd[j].start()
-        add(1, i)
+    for i in range(unit):
+        arrived(3, groups[0][i])
+        over_z3[i].start()
+        arrived(3, groups[1][i])
+        over_z3[unit + i].start()
+    for c in late:
+        c.start()
+    for k in range(CHUNKS):
+        add(0, k, k == 0)
+    for k in groups[0] + groups[1]:
+        add(3, k)
+    for k, j in zip(groups[0], groups[1]):
+        add(1, k)
+        add(2, j)
+    for k, j in zip(groups[1], groups[0]):
+        arrived(1, k)
+        add(1, k)
+        arrived(2, j)
         add(2, j)
     act_copy.wait()
     for c in gq_copies:
         c.wait()
     for d in range(4):
         gq_out[d * blk : (d + 1) * blk, :] = gq_in[d]
-    for i in range(half):
-        fwd[i].wait_recv()
-        add(3, i)
-        fwd[i + half].wait_recv()
-        add(3, i + half)
+    for k, j in zip(groups[2], groups[3]):
+        arrived(1, k)
+        add(1, k)
+        arrived(2, j)
+        add(2, j)
+    for k, j in zip(groups[3], groups[2]):
+        arrived(1, k)
+        add(1, k)
+        arrived(2, j)
+        add(2, j)
+    for k in groups[3][::-1] + groups[2][::-1]:
+        arrived(3, k)
+        add(3, k)
 
     own_rows = acc.shape[1] // (dp_size * 4)
     per_dp = 4 * own_rows
@@ -561,7 +624,7 @@
     ]
     for r in (2, 0, 1):
         t_copies[r].start()
-    for c in to_x + to_y + fwd:
+    for c in early + late + fwd_x + fwd_y + over_z1 + over_z2 + over_z3:
         c.wait_send()
     for c in t_copies:
         c.wait()
@@ -615,7 +678,6 @@
     f32, bf16 = jnp.float32, jnp.bfloat16
     norm_factor = 1.0 / math.sqrt(tokens * 4 * dp_size)
     vmem = pl.BlockSpec(memory_space=pltpu.VMEM)
-    smem = pl.BlockSpec(memory_space=pltpu.SMEM)
     hbm = pl.BlockSpec(memory_space=pl.ANY)
     dma = pltpu.SemaphoreType.DMA
     return pl.pallas_call(
@@ -627,9 +689,13 @@
             jax.ShapeDtypeStruct((own_rows, cols), f32),
             jax.ShapeDtypeStruct((own_rows, wide), f32),
         ),
-        in_specs=[smem, smem, hbm, hbm, hbm, hbm, vmem, vmem, vmem, vmem],
+        in_specs=[hbm] * 10,
         out_specs=[vmem] * 5,
         scratch_shapes=[
+            pltpu.SMEM(doc_lengths.shape, jnp.int32),
+            pltpu.SMEM(block_owner.shape, jnp.int32),
+            pltpu.VMEM((tokens, wide), bf16),
+            pltpu.VMEM((tokens, wide), bf16),
             pltpu.VMEM((2, tokens, width), bf16),
             pltpu.VMEM((4, depth, rank), bf16),
             pltpu.VMEM((4, tokens, HD), bf16),
@@ -648,7 +714,7 @@
             pltpu.VMEM((nz - 1, 2, own_rows, cols), bf16),
             pltpu.VMEM((2, own_rows, cols), f32),
             pltpu.VMEM((own_rows, cols), f32),
-            dma((2,)),
+            dma((8,)),
             dma((6,)),
             dma((6,)),
             dma,
@@ -669,7 +735,7 @@
             dma,
         ],
         compiler_params=pltpu.CompilerParams(
-            collective_id=0, has_side_effects=True, vmem_limit_bytes=48 * 1024 * 1024
+            collective_id=0, has_side_effects=True, vmem_limit_bytes=60 * 1024 * 1024
         ),
         name="fused",
     )(

time: 124 us -> 99.3 us (0.80)
  Pallas kernels: 110 us -> 89.7 us
  local copies, waits for them, and re-layouts: 11.1 us -> 7.42 us
    pallas_call x1, Pallas kernels: 110 us -> 89.7 us  [fused_shards(): pl.pallas_call(functools.partial(fused_kernel, dp_size, norm_factor), out...]
    unnamed x21 -> x5, local copies, waits for them, and re-layouts: 11.1 us -> 7.42 us
where the time goes in v2:
time: 99.3 us; the launch traced here: 97.7 us
  Pallas kernels  89.7 us (90%)
  local copies, waits for them, and re-layouts  7.42 us (7%)
    pallas_call x1, Pallas kernels, fused_shards(): pl.pallas_call(functools.partial(fused_kernel, dp_size, norm_factor), out...  89.7 us
    unnamed x5, local copies, waits for them, and re-layouts  7.42 us

profile of v2, /device:TPU:25, one launch (start us, length us, event | category | flops | bytes accessed | tf_op | source)
XLA Modules:
  0.0 97.7 jit_solution(22902585683185818)
XLA Ops:
  0.6 89.7 %fused.1 = (bf16[128,1024]{1,0:T(8,128)(2,1)}, bf16[128,128]{1,0:T(8,128)(2,1)}, bf16[128,128]{1,0:T(8,128)(2,1)}, f32[16,1280]{1,0:T(8,128)}, f32[16,1024]{1,0:T(8,128)}) custom-call(s32[1,12]{1,0:T(1,128)} %lengths_hbm.1, s32[1,16]{1,0:T(1,128)} %owner_hbm.1, bf16[128,8192]{1,0:T(8,128)(2,1)} %x_hbm.1, bf16[128,8192]{1,0:T(8,128)(2,1)} %g_hbm.1, ...), custom_call_target="tpu_custom_call" | custom-call | tf_op jit(solution)/shard_map/fused/pallas_call | solution.py:683
  90.3 1.7 %copy.20 = bf16[128,1024]{1,0:T(8,128)(2,1)} copy(bf16[128,1024]{1,0:T(8,128)(2,1)} %get-tuple-element.10) | data formatting | bytes 524288
  92.0 1.4 %copy.21 = bf16[128,128]{1,0:T(8,128)(2,1)} copy(bf16[128,128]{1,0:T(8,128)(2,1)} %get-tuple-element.11) | data formatting | bytes 65536
  93.3 1.4 %copy.22 = bf16[128,128]{1,0:T(8,128)(2,1)} copy(bf16[128,128]{1,0:T(8,128)(2,1)} %get-tuple-element.12) | data formatting | bytes 65536
  94.7 1.5 %copy.23 = f32[16,1280]{1,0:T(8,128)} copy(f32[16,1280]{1,0:T(8,128)} %get-tuple-element.13) | data formatting | bytes 163840
  96.2 1.5 %copy.24 = f32[16,1024]{1,0:T(8,128)} copy(f32[16,1024]{1,0:T(8,128)} %get-tuple-element.14) | data formatting | bytes 131072

commit v3 on v2

--- a/solution.py
+++ b/solution.py
@@ -611,35 +611,52 @@
 
     own_rows = acc.shape[1] // (dp_size * 4)
     per_dp = 4 * own_rows
-    for d in range(dp_size):
-        left = acc[:, (d // 2) * 2 * per_dp : (d // 2 + 1) * 2 * per_dp].astype(bf16)
-        if d % 2 == 0:
+    part = dp_size // 2
+    t_copies = []
+    for h in range(2):
+        span = pl.ds(h * part, part)
+        t_copies.append(
+            [
+                remote(
+                    tbuf.at[span, peers[r]],
+                    r1.at[r - 1, span],
+                    t_s.at[3 * h + r - 1],
+                    t_r.at[3 * h + r - 1],
+                    (dp, peers[r]),
+                )
+                for r in (3, 1, 2)
+            ]
+        )
+    for h in range(2):
+        for d in range(h * part, (h + 1) * part, 2):
+            left = acc[:, d * per_dp : (d + 2) * per_dp].astype(bf16)
             both = lax.dot_general(
                 left[:tokens], act[core], down, preferred_element_type=f32
             ) + lax.dot_general(left[tokens:], act_in[...], down, preferred_element_type=f32)
             tbuf[d : d + 2] = both.astype(bf16).reshape(2, 4, own_rows, both.shape[1])
-    t_copies = [
-        remote(tbuf.at[:, peers[r]], r1.at[r - 1], t_s.at[r - 1], t_r.at[r - 1], (dp, peers[r]))
-        for r in (1, 2, 3)
-    ]
-    for r in (2, 0, 1):
-        t_copies[r].start()
+        for c in t_copies[h]:
+            c.start()
     for c in early + late + fwd_x + fwd_y + over_z1 + over_z2 + over_z3:
         c.wait_send()
-    for c in t_copies:
-        c.wait()
-    for d in range(dp_size):
-        total = tbuf[d, me].astype(f32) + r1[0, d].astype(f32)
-        total = total + (r1[1, d].astype(f32) + r1[2, d].astype(f32))
-        s1[d // 2, d % 2] = total.astype(bf16)
     z_copies = [
         remote(
             s1.at[zpeers[k]], r2.at[k - 1], z_s.at[k - 1], z_r.at[k - 1], (2 * zpeers[k] + core, me)
         )
         for k in range(1, nz)
     ]
-    for c in z_copies:
-        c.start()
+    for h in range(2):
+        for c in t_copies[h]:
+            c.wait()
+        for d in range(h * part, (h + 1) * part):
+            total = tbuf[d, me].astype(f32) + r1[0, d].astype(f32)
+            total = total + (r1[1, d].astype(f32) + r1[2, d].astype(f32))
+            s1[d // 2, d % 2] = total.astype(bf16)
+        for k in range(1, nz):
+
+            @pl.when(zpeers[k] // (nz // 2) == h)
+            def _():
+                z_copies[k - 1].start()
+
     for c in z_copies:
         c.wait()
     total = s1[z].astype(f32)
@@ -727,8 +744,8 @@
             dma((3,)),
             dma,
             dma,
-            dma((3,)),
-            dma((3,)),
+            dma((6,)),
+            dma((6,)),
             dma((nz - 1,)),
             dma((nz - 1,)),
             dma,

time: 99.3 us -> 97.5 us (0.982); the launches traced: 97.7 us -> 97.1 us
  no operation moved by 1% of the time
where the time goes in v3:
time: 97.5 us; the launch traced here: 97.1 us
  Pallas kernels  89.1 us (91%)
  local copies, waits for them, and re-layouts  7.42 us (8%)
    pallas_call x1, Pallas kernels, fused_shards(): pl.pallas_call(functools.partial(fused_kernel, dp_size, norm_factor), out...  89.1 us
    unnamed x5, local copies, waits for them, and re-layouts  7.42 us

profile of v3, /device:TPU:25, one launch (start us, length us, event | category | flops | bytes accessed | tf_op | source)
XLA Modules:
  0.0 97.1 jit_solution(12987618238975007907)
XLA Ops:
  0.6 89.1 %fused.1 = (bf16[128,1024]{1,0:T(8,128)(2,1)}, bf16[128,128]{1,0:T(8,128)(2,1)}, bf16[128,128]{1,0:T(8,128)(2,1)}, f32[16,1280]{1,0:T(8,128)}, f32[16,1024]{1,0:T(8,128)}) custom-call(s32[1,12]{1,0:T(1,128)} %lengths_hbm.1, s32[1,16]{1,0:T(1,128)} %owner_hbm.1, bf16[128,8192]{1,0:T(8,128)(2,1)} %x_hbm.1, bf16[128,8192]{1,0:T(8,128)(2,1)} %g_hbm.1, ...), custom_call_target="tpu_custom_call" | custom-call | tf_op jit(solution)/shard_map/fused/pallas_call | solution.py:700
  89.7 1.7 %copy.20 = bf16[128,1024]{1,0:T(8,128)(2,1)} copy(bf16[128,1024]{1,0:T(8,128)(2,1)} %get-tuple-element.10) | data formatting | bytes 524288
  91.4 1.4 %copy.21 = bf16[128,128]{1,0:T(8,128)(2,1)} copy(bf16[128,128]{1,0:T(8,128)(2,1)} %get-tuple-element.11) | data formatting | bytes 65536
  92.8 1.4 %copy.22 = bf16[128,128]{1,0:T(8,128)(2,1)} copy(bf16[128,128]{1,0:T(8,128)(2,1)} %get-tuple-element.12) | data formatting | bytes 65536
  94.1 1.5 %copy.23 = f32[16,1280]{1,0:T(8,128)} copy(f32[16,1280]{1,0:T(8,128)} %get-tuple-element.13) | data formatting | bytes 163840
  95.7 1.5 %copy.24 = f32[16,1024]{1,0:T(8,128)} copy(f32[16,1024]{1,0:T(8,128)} %get-tuple-element.14) | data formatting | bytes 131072

commit v4 on v3

--- a/solution.py
+++ b/solution.py
@@ -611,9 +611,9 @@
 
     own_rows = acc.shape[1] // (dp_size * 4)
     per_dp = 4 * own_rows
-    part = dp_size // 2
+    part = dp_size // 4
     t_copies = []
-    for h in range(2):
+    for h in range(4):
         span = pl.ds(h * part, part)
         t_copies.append(
             [
@@ -627,7 +627,7 @@
                 for r in (3, 1, 2)
             ]
         )
-    for h in range(2):
+    for h in range(4):
         for d in range(h * part, (h + 1) * part, 2):
             left = acc[:, d * per_dp : (d + 2) * per_dp].astype(bf16)
             both = lax.dot_general(
@@ -644,7 +644,7 @@
         )
         for k in range(1, nz)
     ]
-    for h in range(2):
+    for h in range(4):
         for c in t_copies[h]:
             c.wait()
         for d in range(h * part, (h + 1) * part):
@@ -653,7 +653,7 @@
             s1[d // 2, d % 2] = total.astype(bf16)
         for k in range(1, nz):
 
-            @pl.when(zpeers[k] // (nz // 2) == h)
+            @pl.when(zpeers[k] // (nz // 4) == h)
             def _():
                 z_copies[k - 1].start()
 
@@ -744,8 +744,8 @@
             dma((3,)),
             dma,
             dma,
-            dma((6,)),
-            dma((6,)),
+            dma((12,)),
+            dma((12,)),
             dma((nz - 1,)),
             dma((nz - 1,)),
             dma,

time: 97.5 us -> 95.1 us (0.975)
  Pallas kernels: 89.1 us -> 86.7 us
    pallas_call x1, Pallas kernels: 89.1 us -> 86.7 us  [fused_shards(): pl.pallas_call(functools.partial(fused_kernel, dp_size, norm_factor), out...]
where the time goes in v4:
time: 95.1 us; the launch traced here: 94.8 us
  Pallas kernels  86.7 us (91%)
  local copies, waits for them, and re-layouts  7.42 us (8%)
    pallas_call x1, Pallas kernels, fused_shards(): pl.pallas_call(functools.partial(fused_kernel, dp_size, norm_factor), out...  86.7 us
    unnamed x5, local copies, waits for them, and re-layouts  7.42 us

profile of v4, /device:TPU:25, one launch (start us, length us, event | category | flops | bytes accessed | tf_op | source)
XLA Modules:
  0.0 94.8 jit_solution(3986342785559757326)
XLA Ops:
  0.6 86.7 %fused.1 = (bf16[128,1024]{1,0:T(8,128)(2,1)}, bf16[128,128]{1,0:T(8,128)(2,1)}, bf16[128,128]{1,0:T(8,128)(2,1)}, f32[16,1280]{1,0:T(8,128)}, f32[16,1024]{1,0:T(8,128)}) custom-call(s32[1,12]{1,0:T(1,128)} %lengths_hbm.1, s32[1,16]{1,0:T(1,128)} %owner_hbm.1, bf16[128,8192]{1,0:T(8,128)(2,1)} %x_hbm.1, bf16[128,8192]{1,0:T(8,128)(2,1)} %g_hbm.1, ...), custom_call_target="tpu_custom_call" | custom-call | tf_op jit(solution)/shard_map/fused/pallas_call | solution.py:700
  87.3 1.7 %copy.20 = bf16[128,1024]{1,0:T(8,128)(2,1)} copy(bf16[128,1024]{1,0:T(8,128)(2,1)} %get-tuple-element.10) | data formatting | bytes 524288
  89.0 1.4 %copy.21 = bf16[128,128]{1,0:T(8,128)(2,1)} copy(bf16[128,128]{1,0:T(8,128)(2,1)} %get-tuple-element.11) | data formatting | bytes 65536
  90.4 1.4 %copy.22 = bf16[128,128]{1,0:T(8,128)(2,1)} copy(bf16[128,128]{1,0:T(8,128)(2,1)} %get-tuple-element.12) | data formatting | bytes 65536
  91.8 1.5 %copy.23 = f32[16,1280]{1,0:T(8,128)} copy(f32[16,1280]{1,0:T(8,128)} %get-tuple-element.13) | data formatting | bytes 163840
  93.3 1.5 %copy.24 = f32[16,1024]{1,0:T(8,128)} copy(f32[16,1024]{1,0:T(8,128)} %get-tuple-element.14) | data formatting | bytes 131072
